TPU v7x, 512 devices: a whole 4x8x8 slice. The times are simulated.
512 devices in a mesh: rx: 32 (over z, y_lo, core), freq: 16 (over y_hi, x).
Axes of the slice: x: 4, y: 8 (y_hi: 4, y_lo: 2; y = y_hi * 2 + y_lo), z: 8, core: 2. Of those that a mesh axis runs over, the one named last changes fastest.
Arguments:
- spectra: bfloat16 [2, 128, 32, 8192], P(None, 'freq', None, 'rx'), may hold values from -60 to 60
- source_block: int32 [1], replicated, may hold values from 0 to 31
Outputs:
- correlations: bfloat16 [256, 256, 8192], P(None, 'freq', 'rx')
All inputs are finite; a program needn't handle non-finite values.
Results may differ from a plain program's by a relative error of at most 0.0057.
Values may be sent and summed in bfloat16 or wider, within the bound.
A program may use at most 64 MiB of HBM per device.

v0:
```python
import math
import jax
import jax.numpy as jnp
from jax import lax
from jax.sharding import PartitionSpec as P

F = 128
W = 32
LAGS = 256


def extended(cells, sides, width):
    for axis, dim in sides:
        count = lax.axis_size(axis)
        ends = count - 1
        head = lax.slice_in_dim(cells, 0, width, axis=dim)
        tail = lax.slice_in_dim(cells, cells.shape[dim] - width, cells.shape[dim], axis=dim)
        cells = jnp.concatenate(
            [
                lax.ppermute(tail, axis, [(i, (i + 1) % count) for i in range(ends)]),
                cells,
                lax.ppermute(head, axis, [((i + 1) % count, i) for i in range(ends)]),
            ],
            axis=dim,
        )
    return cells


def broadcast(value, axis, source):
    kept = jnp.where(lax.axis_index(axis) == source, value, 0).astype(value.dtype)
    return lax.psum(kept, axis)


def whiten(planes_in):
    planes = planes_in.astype(jnp.float32)
    magnitude = jnp.sqrt(planes[0] * planes[0] + planes[1] * planes[1])
    padded = extended(magnitude, (("freq", 0),), 1)
    smooth = (padded[:-2] + padded[1:-1] + padded[2:]) / 3.0
    divisor = jnp.maximum(smooth, 0.5)
    return (planes / divisor[None]).astype(jnp.bfloat16)


def build_lag_basis():
    bins = jnp.arange(F, dtype=jnp.int32)
    lagged = jnp.arange(LAGS, dtype=jnp.int32)
    phase = bins[:, None] * lagged[None, :] % LAGS
    angle = phase.astype(jnp.float32) * (2.0 * math.pi / LAGS)
    return jnp.concatenate([jnp.cos(angle), -jnp.sin(angle)], axis=0).astype(jnp.bfloat16)


def window_products(sent, white):
    joined_sources = jnp.concatenate([sent[0], sent[1]], axis=1)
    leading_operand = jnp.concatenate([white[0], white[1]], axis=1)
    trailing_operand = jnp.concatenate([white[1], -white[0]], axis=1)
    real_total = jnp.einsum(
        "pgo,pgd->pod", joined_sources, leading_operand, preferred_element_type=jnp.float32
    )
    imaginary_total = jnp.einsum(
        "pgo,pgd->pod", joined_sources, trailing_operand, preferred_element_type=jnp.float32
    )
    return (real_total, imaginary_total)


def transform(cross_part, basis_table):
    stacked = cross_part.reshape(2 * F, cross_part.shape[2], cross_part.shape[3])
    lagged = jnp.einsum("kl,ksr->slr", basis_table, stacked, preferred_element_type=jnp.float32) * (
        2.0 / F
    )
    return lagged.astype(jnp.bfloat16)


def on_device(spectra, source_block):
    white = whiten(spectra)
    owner = source_block[0]
    sent = broadcast(white, "rx", owner)
    real_total, imaginary_total = window_products(sent, white)
    cross = (jnp.stack([real_total, imaginary_total]) / W).astype(jnp.bfloat16)
    basis_table = build_lag_basis()
    spread = lax.all_to_all(cross, "freq", split_axis=2, concat_axis=1, tiled=True)
    lagged = transform(spread, basis_table)
    result = lax.all_to_all(lagged, "freq", split_axis=1, concat_axis=0, tiled=True)
    return result


def solution(mesh):
    in_specs = (P(None, "freq", None, "rx"), P())
    out_specs = P(None, "freq", "rx")
    return jax.shard_map(
        on_device, mesh=mesh, in_specs=in_specs, out_specs=out_specs, check_vma=False
    )
```

profile of v0, /device:TPU:1, one launch (start us, length us, event | category | flops | bytes accessed | tf_op | source)
XLA Modules:
  0.0 392.1 jit_solution(4345271281972983025)
XLA Ops:
  6.5 0.0 copy-start
  6.5 0.0 all-reduce.2.cloned.1.call-start
  6.5 1.1 convert_element_type.23
  7.6 0.1 fusion.10
  7.7 3.9 %collective-permute-start = (f32[1,32,256]{2,1,0:T(8,128)S(1)}, f32[1,32,256]{2,1,0:T(8,128)S(1)}, u32[]{:S(2)}, u32[]{:S(2)}) collective-permute-start(f32[1,32,256]{2,1,0:T(8,128)S(1)} %get-tuple-element.11), channel_id=1, source_target_pairs={{0,1},{1,2},{2,3},{3,4},{4,5},{5,6},{6,7},{7,8},{8,9},{9,10},{10,1... | collective-permute-start | bytes 98312 | tf_op jit(solution)/shard_map/ppermute | solution.py:20
  11.7 1.3 collective-permute-start.1
  13.0 0.1 fusion.29
  13.7 0.0 collective-permute-done
  13.7 2.6 collective-permute-done.1
  16.4 0.0 copy-done
  16.4 0.8 broadcast_select_fusion
  17.2 0.0 all-reduce.2.cloned.1.call-update
  17.3 237.6 %all-reduce.2.cloned.1.call-done = bf16[2,8,32,256]{3,2,1,0:T(8,128)(2,1)} async-done(((bf16[2,8,32,256]{3,2,1,0:T(8,128)(2,1)}), bf16[2,8,32,256]{3,2,1,0:T(8,128)(2,1)}) %all-reduce.2.cloned.1.call-update) | async-done | bytes 262160 | tf_op jit(solution)/shard_map/psum | solution.py:31
  254.9 1.0 slice_bitcast_fusion.3
  255.8 0.5 convolution_bitcast_fusion.1
  256.3 0.5 convolution_bitcast_fusion
  256.8 0.5 fusion
  257.3 2.5 copy.17
  259.8 8.1 %all-to-all-start = ((bf16[2,8,256,256]{3,1,0,2:T(8,128)(2,1)}), bf16[2,8,256,256]{3,1,0,2:T(8,128)(2,1)S(1)}, u32[]{:S(2)}, u32[]{:S(2)}) async-start(bf16[2,8,256,256]{3,1,0,2:T(8,128)(2,1)} %copy.17), calls=%async_computation | async-start | bytes 4194304 | tf_op jit(solution)/shard_map/all_to_all | solution.py:79
  267.9 0.5 negate_convert_fusion
  268.4 52.8 %all-to-all-done = bf16[2,8,256,256]{3,1,0,2:T(8,128)(2,1)S(1)} async-done(((bf16[2,8,256,256]{3,1,0,2:T(8,128)(2,1)}), bf16[2,8,256,256]{3,1,0,2:T(8,128)(2,1)S(1)}, u32[]{:S(2)}, u32[]{:S(2)}) %all-to-all-start) | async-done | bytes 2097184 | tf_op jit(solution)/shard_map/all_to_all | solution.py:79
  321.3 0.7 copy.19
  322.0 3.0 fusion.2
  325.0 3.3 copy.21
  328.3 54.7 %all_to_all.33 = bf16[16,256,256]{2,0,1:T(8,128)(2,1)S(1)} all-to-all(bf16[16,256,256]{2,0,1:T(8,128)(2,1)S(1)} %copy.21), channel_id=1, replica_groups=mesh['rx'=32,'freq'=16] {'freq'}, dimensions={1} | all-to-all | bytes 4194304 | tf_op jit(solution)/shard_map/all_to_all | solution.py:81
  383.1 2.2 copy.23
  (4 shorter events, 0.1 us)
Async XLA Ops:
  6.5 9.8 %copy-start = (bf16[2,8,32,256]{3,2,1,0:T(8,128)(2,1)S(1)}, bf16[2,8,32,256]{3,2,1,0:T(8,128)(2,1)}, u32[]{:S(2)}) copy-start(bf16[2,8,32,256]{3,2,1,0:T(8,128)(2,1)} %param.2) | copy-start | bytes 786436
  6.5 248.3 %all-reduce.2.cloned.1.call-start = ((), (), s32[]{:S(2)}) async-start(), calls=%async_computation.2 | async-start | bytes 524288 | tf_op jit(solution)/shard_map/psum | solution.py:31
  7.7 6.0 %collective-permute-start = (f32[1,32,256]{2,1,0:T(8,128)S(1)}, f32[1,32,256]{2,1,0:T(8,128)S(1)}, u32[]{:S(2)}, u32[]{:S(2)}) collective-permute-start(f32[1,32,256]{2,1,0:T(8,128)S(1)} %get-tuple-element.11), channel_id=1, source_target_pairs={{0,1},{1,2},{2,3},{3,4},{4,5},{5,6},{6,7},{7,8},{8,9},{9,10},{10,1... | collective-permute-start | bytes 98312 | tf_op jit(solution)/shard_map/ppermute | solution.py:20
  11.7 4.7 %collective-permute-start.1 = (f32[1,32,256]{2,1,0:T(8,128)S(1)}, f32[1,32,256]{2,1,0:T(8,128)S(1)}, u32[]{:S(2)}, u32[]{:S(2)}) collective-permute-start(f32[1,32,256]{2,1,0:T(8,128)S(1)} %get-tuple-element.12), channel_id=1, source_target_pairs={{1,0},{2,1},{3,2},{4,3},{5,4},{6,5},{7,6},{8,7},{9,8},{10,9},{11,1... | collective-permute-start | bytes 98312 | tf_op jit(solution)/shard_map/ppermute | solution.py:22
  259.8 61.5 %all-to-all-start = ((bf16[2,8,256,256]{3,1,0,2:T(8,128)(2,1)}), bf16[2,8,256,256]{3,1,0,2:T(8,128)(2,1)S(1)}, u32[]{:S(2)}, u32[]{:S(2)}) async-start(bf16[2,8,256,256]{3,1,0,2:T(8,128)(2,1)} %copy.17), calls=%async_computation | async-start | bytes 4194304 | tf_op jit(solution)/shard_map/all_to_all | solution.py:79
Sparse Core Ops, SparseCore 0:
  17.4 237.4 all-reduce.1
where the time goes:
time: 392 us
  waiting for transfers between devices  293 us (75%)
  blocking collectives  54.7 us (14%)
  between operations  14.2 us (4%)
  starting transfers between devices  13.3 us (3%)
  local copies, waits for them, and re-layouts  9.73 us (2%)
  matrix products  4 us (1%)
    psum x1, waiting for transfers between devices, broadcast(): return lax.psum(kept, axis)  238 us
    all_to_all x1, blocking collectives, on_device(): lax.all_to_all(lagged, 'freq', split_axis=1, concat_axis=0, tiled=True)  54.7 us
    all_to_all x1, waiting for transfers between devices, on_device(): lax.all_to_all(cross, 'freq', split_axis=2, concat_axis=1, tiled=True)  52.8 us
    all_to_all x1, starting transfers between devices, on_device(): lax.all_to_all(cross, 'freq', split_axis=2, concat_axis=1, tiled=True)  8.08 us
  transfers between devices with their start and end apart: 4, of which 3 were waited for; matrix products, arithmetic and copies ran while one was open for 0% of the time, Pallas kernels for 0%

commit v1 on v0

--- a/solution.py
+++ b/solution.py
@@ -28,7 +28,7 @@
 
 def broadcast(value, axis, source):
     kept = jnp.where(lax.axis_index(axis) == source, value, 0).astype(value.dtype)
-    return lax.psum(kept, axis)
+    return jnp.sum(lax.all_gather(kept, axis), axis=0)
 
 
 def whiten(planes_in):

time: 392 us -> 246 us (0.63)
  waiting for transfers between devices: 293 us -> 140 us
  other arithmetic: 3.15 us -> 8.71 us
    psum x1 -> x0, waiting for transfers between devices: 238 us -> none  [broadcast(): return lax.psum(kept, axis)]
    all_gather x0 -> x1, waiting for transfers between devices: none -> 85.4 us  [broadcast(): return jnp.sum(lax.all_gather(kept, axis), axis=0)]
    reduce_sum x0 -> x1, other arithmetic: none -> 5.56 us  [broadcast(): return jnp.sum(lax.all_gather(kept, axis), axis=0)]
where the time goes in v1:
time: 246 us
  waiting for transfers between devices  140 us (57%)
  blocking collectives  55.6 us (23%)
  starting transfers between devices  14.2 us (6%)
  between operations  14.2 us (6%)
  local copies, waits for them, and re-layouts  8.76 us (4%)
  other arithmetic  8.71 us (4%)
  matrix products  4.01 us (2%)
    all_gather x1, waiting for transfers between devices, broadcast(): return jnp.sum(lax.all_gather(kept, axis), axis=0)  85.4 us
    all_to_all x1, blocking collectives, on_device(): lax.all_to_all(lagged, 'freq', split_axis=1, concat_axis=0, tiled=True)  55.6 us
    all_to_all x1, waiting for transfers between devices, on_device(): lax.all_to_all(cross, 'freq', split_axis=2, concat_axis=1, tiled=True)  52.1 us
    all_to_all x1, starting transfers between devices, on_device(): lax.all_to_all(cross, 'freq', split_axis=2, concat_axis=1, tiled=True)  8.97 us
    reduce_sum x1, other arithmetic, broadcast(): return jnp.sum(lax.all_gather(kept, axis), axis=0)  5.56 us
  transfers between devices with their start and end apart: 4, of which 3 were waited for; matrix products, arithmetic and copies ran while one was open for 0% of the time, Pallas kernels for 0%

profile of v1, /device:TPU:1, one launch (start us, length us, event | category | flops | bytes accessed | tf_op | source)
XLA Modules:
  0.0 245.5 jit_solution(8558948940073464919)
XLA Ops:
  6.5 0.0 copy-start
  6.5 0.0 all-gather.3.cloned.1.call-start
  6.5 1.1 convert_element_type.25
  7.6 0.1 fusion.10
  7.7 3.9 %collective-permute-start = (f32[1,32,256]{2,1,0:T(8,128)S(1)}, f32[1,32,256]{2,1,0:T(8,128)S(1)}, u32[]{:S(2)}, u32[]{:S(2)}) collective-permute-start(f32[1,32,256]{2,1,0:T(8,128)S(1)} %get-tuple-element.11), channel_id=1, source_target_pairs={{0,1},{1,2},{2,3},{3,4},{4,5},{5,6},{6,7},{7,8},{8,9},{9,10},{10,1... | collective-permute-start | bytes 98312 | tf_op jit(solution)/shard_map/ppermute | solution.py:20
  11.7 1.3 collective-permute-start.1
  13.0 0.1 fusion.29
  13.7 0.0 collective-permute-done
  13.7 2.6 %collective-permute-done.1 = f32[1,32,256]{2,1,0:T(8,128)S(1)} collective-permute-done((f32[1,32,256]{2,1,0:T(8,128)S(1)}, f32[1,32,256]{2,1,0:T(8,128)S(1)}, u32[]{:S(2)}, u32[]{:S(2)}) %collective-permute-start.1) | collective-permute-done | bytes 32800 | tf_op jit(solution)/shard_map/ppermute | solution.py:22
  16.4 0.0 copy-done
  16.4 0.8 broadcast_select_fusion
  17.2 0.0 all-gather.3.cloned.1.call-update
  17.3 85.4 %all-gather.3.cloned.1.call-done = bf16[64,8,32,256]{3,2,1,0:T(8,128)(2,1)} async-done(((bf16[2,8,32,256]{3,2,1,0:T(8,128)(2,1)}), bf16[64,8,32,256]{3,2,1,0:T(8,128)(2,1)}) %all-gather.3.cloned.1.call-update) | async-done | bytes 8388624 | tf_op jit(solution)/shard_map/all_gather | solution.py:31
  102.6 5.6 %reduce_sum.12 = bf16[2,8,32,256]{3,2,1,0:T(8,128)(2,1)S(1)} reduce(bf16[32,2,8,32,256]{4,3,2,1,0:T(8,128)(2,1)} %bitcast.36, bf16[]{:T(256)} %constant.31.clone.1), dimensions={0}, to_apply=%region_0.1 | reduce | flops 4063232 | bytes 8650754 | tf_op jit(solution)/shard_map/reduce_sum | solution.py:31
  108.2 0.5 convolution_bitcast_fusion.1
  108.7 0.5 convolution_bitcast_fusion
  109.2 0.5 fusion
  109.7 2.5 %copy.17 = bf16[2,8,256,256]{3,1,0,2:T(8,128)(2,1)} copy(bf16[2,8,256,256]{3,2,1,0:T(8,128)(2,1)S(1)} %fusion) | data formatting | bytes 4194304 | tf_op jit(solution)/shard_map/convert_element_type | solution.py:77
  112.2 9.0 %all-to-all-start = ((bf16[2,8,256,256]{3,1,0,2:T(8,128)(2,1)}), bf16[2,8,256,256]{3,1,0,2:T(8,128)(2,1)S(1)}, u32[]{:S(2)}, u32[]{:S(2)}) async-start(bf16[2,8,256,256]{3,1,0,2:T(8,128)(2,1)} %copy.17), calls=%async_computation | async-start | bytes 4194304 | tf_op jit(solution)/shard_map/all_to_all | solution.py:79
  121.2 0.5 negate_convert_fusion
  121.7 52.1 %all-to-all-done = bf16[2,8,256,256]{3,1,0,2:T(8,128)(2,1)S(1)} async-done(((bf16[2,8,256,256]{3,1,0,2:T(8,128)(2,1)}), bf16[2,8,256,256]{3,1,0,2:T(8,128)(2,1)S(1)}, u32[]{:S(2)}, u32[]{:S(2)}) %all-to-all-start) | async-done | bytes 2097184 | tf_op jit(solution)/shard_map/all_to_all | solution.py:79
  173.8 0.7 copy.19
  174.5 3.0 %fusion.2 = bf16[16,256,256]{1,2,0:T(8,128)(2,1)} fusion(bf16[256,16,256]{2,1,0:T(8,128)(2,1)S(1)} %bitcast.39, bf16[128,256]{1,0:T(8,128)(2,1)S(1)} %get-tuple-element.13, bf16[128,256]{1,0:T(8,128)(2,1)S(1)} %get-tuple-element.14), kind=kOutput, calls=%fused_computation.4 | convolution fusion | flops 539230208 | bytes 4325376 | tf_op jit(solution)/shard_map/kl,ksr->slr/dot_general | solution.py:66
  177.5 3.3 %copy.21 = bf16[16,256,256]{2,0,1:T(8,128)(2,1)S(1)} copy(bf16[16,256,256]{1,2,0:T(8,128)(2,1)} %fusion.2) | data formatting | bytes 4194304 | tf_op jit(solution)/shard_map/convert_element_type | solution.py:69
  180.9 55.6 %all_to_all.33 = bf16[16,256,256]{2,0,1:T(8,128)(2,1)S(1)} all-to-all(bf16[16,256,256]{2,0,1:T(8,128)(2,1)S(1)} %copy.21), channel_id=1, replica_groups=mesh['rx'=32,'freq'=16] {'freq'}, dimensions={1} | all-to-all | bytes 4194304 | tf_op jit(solution)/shard_map/all_to_all | solution.py:81
  236.5 2.2 copy.23
  (5 shorter events, 0.1 us)
Async XLA Ops:
  6.5 9.8 %copy-start = (bf16[2,8,32,256]{3,2,1,0:T(8,128)(2,1)S(1)}, bf16[2,8,32,256]{3,2,1,0:T(8,128)(2,1)}, u32[]{:S(2)}) copy-start(bf16[2,8,32,256]{3,2,1,0:T(8,128)(2,1)} %param.2) | copy-start | bytes 786436
  6.5 96.1 %all-gather.3.cloned.1.call-start = ((), (), s32[]{:S(2)}) async-start(), calls=%async_computation.2 | async-start | bytes 8650752 | tf_op jit(solution)/shard_map/all_gather | solution.py:31
  7.7 6.0 %collective-permute-start = (f32[1,32,256]{2,1,0:T(8,128)S(1)}, f32[1,32,256]{2,1,0:T(8,128)S(1)}, u32[]{:S(2)}, u32[]{:S(2)}) collective-permute-start(f32[1,32,256]{2,1,0:T(8,128)S(1)} %get-tuple-element.11), channel_id=1, source_target_pairs={{0,1},{1,2},{2,3},{3,4},{4,5},{5,6},{6,7},{7,8},{8,9},{9,10},{10,1... | collective-permute-start | bytes 98312 | tf_op jit(solution)/shard_map/ppermute | solution.py:20
  11.7 4.7 %collective-permute-start.1 = (f32[1,32,256]{2,1,0:T(8,128)S(1)}, f32[1,32,256]{2,1,0:T(8,128)S(1)}, u32[]{:S(2)}, u32[]{:S(2)}) collective-permute-start(f32[1,32,256]{2,1,0:T(8,128)S(1)} %get-tuple-element.12), channel_id=1, source_target_pairs={{1,0},{2,1},{3,2},{4,3},{5,4},{6,5},{7,6},{8,7},{9,8},{10,9},{11,1... | collective-permute-start | bytes 98312 | tf_op jit(solution)/shard_map/ppermute | solution.py:22
  112.2 61.6 %all-to-all-start = ((bf16[2,8,256,256]{3,1,0,2:T(8,128)(2,1)}), bf16[2,8,256,256]{3,1,0,2:T(8,128)(2,1)S(1)}, u32[]{:S(2)}, u32[]{:S(2)}) async-start(bf16[2,8,256,256]{3,1,0,2:T(8,128)(2,1)} %copy.17), calls=%async_computation | async-start | bytes 4194304 | tf_op jit(solution)/shard_map/all_to_all | solution.py:79
Sparse Core Ops, SparseCore 0:
  17.4 85.2 all-gather.2
